TPU v7x, 32 devices: a whole 2x2x4 slice. The times are simulated.
32 devices in a mesh: stretch: 8 (over z, y), head: 2 (over x), cfg: 2 (over core).
Axes of the slice: x: 2, y: 2, z: 4, core: 2. Of those that a mesh axis runs over, the one named last changes fastest.
Arguments:
- queries: bfloat16 [14336, 5120], P(('cfg', 'stretch', 'head')), parts along dimension 0, may hold values from -6 to 6
- keys: bfloat16 [14336, 5120], P(('cfg', 'stretch', 'head')), parts along dimension 0, may hold values from -6 to 6
- values: bfloat16 [14336, 5120], P(('cfg', 'stretch', 'head')), parts along dimension 0, may hold values from -6 to 6
- frames: int32 [8], replicated, may hold values from 4 to 7, as said below
- motion: int32 [8], replicated, may hold values from 0 to 4, as said below
Outputs:
- attended: bfloat16 [14336, 5120], P(('cfg', 'stretch', 'head')), parts along dimension 0
There are 2 independent parts, one for each index of `cfg`. A program takes and returns all parts, laid end to end along the dimension named above; an argument that names none is the same for every part. Nothing has to cross between parts.
Inputs may be any that keep to these rules, and one draw needn't show every extreme that they name: Every stretch holds at least 4 frames; some stretch holds 7. `motion`: stretch 0 takes none; some stretch takes 4.
All inputs are finite; a program needn't handle non-finite values.
Results may differ from a plain program's by a relative error of at most 0.0046.
Values may be sent and summed in bfloat16 or wider, within the bound.
A program may use at most 128 MiB of HBM per device.

v0:
```python
import math

import jax
import jax.numpy as jnp
from jax import lax
from jax.sharding import PartitionSpec as P

HD = 128
FT = 128
MOT_CAP = 4


NEG = -1e30


def from_behind(shard, axis, by):
    size = lax.axis_size(axis)
    pairs = [(i, i + by) for i in range(size) if 0 <= i + by < size]
    return lax.ppermute(shard, axis, pairs)


def head_block(q_head, k_head, v_head, key_live):
    scores = lax.dot_general(
        q_head, k_head, (((1,), (1,)), ((), ())), preferred_element_type=jnp.float32
    )
    scores = scores * (1.0 / math.sqrt(q_head.shape[1]))
    masked = jnp.where(key_live[None, :], scores, NEG)
    top = jnp.max(masked, axis=1)
    weights = jnp.where(key_live[None, :], jnp.exp(masked - top[:, None]), 0.0)
    total = jnp.sum(weights, axis=1)
    acc = jnp.dot(weights.astype(jnp.bfloat16), v_head, preferred_element_type=jnp.float32)
    return (top, total, acc)


def pick_head(array, index):
    return lax.dynamic_index_in_dim(array, index, 1, keepdims=False)


def own_part(queries, keys, values, key_live):
    rows, count, width = queries.shape
    start = (
        jnp.zeros((rows, count), jnp.float32),
        jnp.zeros((rows, count), jnp.float32),
        jnp.zeros((rows, count, width), jnp.float32),
    )

    def own_step(index, carry):
        tops, totals, accs = carry
        top, total, acc = head_block(
            pick_head(queries, index), pick_head(keys, index), pick_head(values, index), key_live
        )
        tops = lax.dynamic_update_index_in_dim(tops, top, index, 1)
        totals = lax.dynamic_update_index_in_dim(totals, total, index, 1)
        accs = lax.dynamic_update_index_in_dim(accs, acc, index, 1)
        return (tops, totals, accs)

    return lax.fori_loop(0, count, own_step, start)


def finish(queries, motion_keys, motion_values, motion_live, query_live, partial_value):
    tops, totals, accs = partial_value
    count = queries.shape[1]

    def finish_step(index, result):
        top, total, acc = head_block(
            pick_head(queries, index),
            pick_head(motion_keys, index),
            pick_head(motion_values, index),
            motion_live,
        )
        top_own = pick_head(tops, index)
        total_own = pick_head(totals, index)
        acc_own = pick_head(accs, index)
        peak = jnp.maximum(top_own, top)
        factor_own = jnp.exp(top_own - peak)
        factor_mot = jnp.exp(top - peak)
        mixed = (acc_own * factor_own[:, None] + acc * factor_mot[:, None]) / (
            total_own * factor_own + total * factor_mot
        )[:, None]
        mixed = jnp.where(query_live[:, None], mixed, 0.0).astype(jnp.bfloat16)
        return lax.dynamic_update_index_in_dim(result, mixed, index, 1)

    return lax.fori_loop(0, count, finish_step, jnp.zeros(queries.shape, jnp.bfloat16))


def body(queries, keys, values, frames, motion):
    rows, width = queries.shape
    groups = lax.axis_size("head")
    stretch_index = lax.axis_index("stretch")
    span = rows * groups
    tail = MOT_CAP * FT
    local = width // groups
    count_own = frames[stretch_index]
    spot = jnp.arange(span, dtype=jnp.int32) // FT
    slot = jnp.arange(tail, dtype=jnp.int32) // FT
    live = spot < count_own
    motion_live = slot >= MOT_CAP - motion[stretch_index]
    tail_begin = (count_own - MOT_CAP) * FT
    q_heads, k_heads, v_heads = (
        lax.all_to_all(queries, "head", split_axis=1, concat_axis=0, tiled=True),
        lax.all_to_all(keys, "head", split_axis=1, concat_axis=0, tiled=True),
        lax.all_to_all(values, "head", split_axis=1, concat_axis=0, tiled=True),
    )
    k_tail = lax.dynamic_slice_in_dim(k_heads, tail_begin, tail, 0)
    v_tail = lax.dynamic_slice_in_dim(v_heads, tail_begin, tail, 0)
    k_prior, v_prior = from_behind((k_tail, v_tail), "stretch", 1)
    count = local // HD
    q_shaped = q_heads.reshape(span, count, HD)
    partial_value = own_part(
        q_shaped, k_heads.reshape(span, count, HD), v_heads.reshape(span, count, HD), live
    )
    mixed = finish(
        q_shaped,
        k_prior.reshape(tail, count, HD),
        v_prior.reshape(tail, count, HD),
        motion_live,
        live,
        partial_value,
    )
    result = lax.all_to_all(
        mixed.reshape(span, local), "head", split_axis=0, concat_axis=1, tiled=True
    )
    return result


def solution(mesh):
    placed = (
        P(("cfg", "stretch", "head"), None),
        P(("cfg", "stretch", "head"), None),
        P(("cfg", "stretch", "head"), None),
        P(),
        P(),
    )
    return jax.shard_map(
        body,
        mesh=mesh,
        in_specs=placed,
        out_specs=P(("cfg", "stretch", "head"), None),
        check_vma=False,
    )
```

profile of v0, /device:TPU:0, one launch (start us, length us, event | category | flops | bytes accessed | tf_op | source)
XLA Modules:
  0.0 536.3 jit_solution(4850194006780771079)
XLA Ops:
  0.0 4.8 copy.70
  4.8 5.8 %all-to-all-start.1 = ((bf16[448,2,2560]{2,0,1:T(8,128)(2,1)}), bf16[448,2,2560]{2,0,1:T(8,128)(2,1)}, u32[]{:S(2)}, u32[]{:S(2)}) async-start(bf16[448,2,2560]{2,0,1:T(8,128)(2,1)} %bitcast.86), calls=%async_computation.1 | async-start | bytes 9175040 | tf_op jit(solution)/shard_map/all_to_all | solution.py:101
  10.6 4.7 copy.69
  15.3 48.3 %all-to-all-done.1 = bf16[448,2,2560]{2,0,1:T(8,128)(2,1)} async-done(((bf16[448,2,2560]{2,0,1:T(8,128)(2,1)}), bf16[448,2,2560]{2,0,1:T(8,128)(2,1)}, u32[]{:S(2)}, u32[]{:S(2)}) %all-to-all-start.1) | async-done | bytes 4587552 | tf_op jit(solution)/shard_map/all_to_all | solution.py:101
  63.6 5.7 %all-to-all-start.2 = ((bf16[448,2,2560]{2,0,1:T(8,128)(2,1)}), bf16[448,2,2560]{2,0,1:T(8,128)(2,1)}, u32[]{:S(2)}, u32[]{:S(2)}) async-start(bf16[448,2,2560]{2,0,1:T(8,128)(2,1)} %bitcast.85), calls=%async_computation.2 | async-start | bytes 9175040 | tf_op jit(solution)/shard_map/all_to_all | solution.py:102
  69.3 4.8 copy.71
  74.2 46.5 %all-to-all-done.2 = bf16[448,2,2560]{2,0,1:T(8,128)(2,1)} async-done(((bf16[448,2,2560]{2,0,1:T(8,128)(2,1)}), bf16[448,2,2560]{2,0,1:T(8,128)(2,1)}, u32[]{:S(2)}, u32[]{:S(2)}) %all-to-all-start.2) | async-done | bytes 4587552 | tf_op jit(solution)/shard_map/all_to_all | solution.py:102
  120.6 5.8 %all-to-all-start = ((bf16[448,2,2560]{2,0,1:T(8,128)(2,1)}), bf16[448,2,2560]{2,0,1:T(8,128)(2,1)}, u32[]{:S(2)}, u32[]{:S(2)}) async-start(bf16[448,2,2560]{2,0,1:T(8,128)(2,1)} %bitcast.84), calls=%async_computation | async-start | bytes 9175040 | tf_op jit(solution)/shard_map/all_to_all | solution.py:100
  131.0 4.9 collective-permute-start
  135.8 3.4 constant_dynamic-slice_fusion.2
  139.2 3.6 collective-permute-start.1
  142.8 34.1 %all-to-all-done = bf16[448,2,2560]{2,0,1:T(8,128)(2,1)} async-done(((bf16[448,2,2560]{2,0,1:T(8,128)(2,1)}), bf16[448,2,2560]{2,0,1:T(8,128)(2,1)}, u32[]{:S(2)}, u32[]{:S(2)}) %all-to-all-start) | async-done | bytes 4587552 | tf_op jit(solution)/shard_map/all_to_all | solution.py:100
  176.9 8.7 %reshape.51 = bf16[896,20,128]{2,1,0:T(8,128)(2,1)} reshape(bf16[2,448,2560]{2,1,0:T(8,128)(2,1)} %bitcast) | data formatting | bytes 9175040 | tf_op jit(solution)/shard_map/reshape | solution.py:108
  185.6 5.6 %copy.50 = bf16[896,20,128]{2,0,1:T(8,128)(2,1)} copy(bf16[896,20,128]{2,1,0:T(8,128)(2,1)} %reshape.51) | data formatting | bytes 9175040
  191.2 8.7 %reshape.52 = bf16[896,20,128]{2,1,0:T(8,128)(2,1)} reshape(bf16[2,448,2560]{2,1,0:T(8,128)(2,1)} %bitcast.1) | data formatting | bytes 9175040 | tf_op jit(solution)/shard_map/reshape | solution.py:110
  200.0 5.7 %copy.51 = bf16[896,20,128]{2,0,1:T(8,128)(2,1)} copy(bf16[896,20,128]{2,1,0:T(8,128)(2,1)} %reshape.52) | data formatting | bytes 9175040
  205.7 8.7 %reshape.53 = bf16[896,20,128]{2,1,0:T(8,128)(2,1)} reshape(bf16[2,448,2560]{2,1,0:T(8,128)(2,1)} %bitcast.2) | data formatting | bytes 9175040 | tf_op jit(solution)/shard_map/reshape | solution.py:110
  214.5 5.7 %copy.52 = bf16[896,20,128]{2,0,1:T(8,128)(2,1)} copy(bf16[896,20,128]{2,1,0:T(8,128)(2,1)} %reshape.53) | data formatting | bytes 9175040
  220.2 125.8 %while.32 = (s32[]{:T(128)}, f32[896,20]{0,1:T(8,128)S(1)}, f32[896,20]{0,1:T(8,128)S(1)}, f32[896,20,128]{2,0,1:T(8,128)}, bf16[896,20,128]{2,0,1:T(8,128)(2,1)...) while((s32[]{:T(128)}, f32[896,20]{0,1:T(8,128)S(1)}, ...), condition=%wide.region_3.4_spmd.clone, body=%wide.region_0.3_spmd.clone.sunk | while | flops 421484672 | bytes 10829425 | solution.py:57
  222.5 2.9 fusion.91
  228.8 2.9 fusion.91
  235.1 2.9 fusion.91
  241.4 2.9 fusion.91
  247.7 2.9 fusion.91
  254.0 2.9 fusion.91
  260.3 2.9 fusion.91
  266.6 2.9 fusion.91
  272.8 2.9 fusion.91
  279.1 2.9 fusion.91
  285.4 2.8 fusion.91
  291.7 2.9 fusion.91
  298.0 2.9 fusion.91
  304.3 2.8 fusion.91
  310.6 2.9 fusion.91
  316.9 2.9 fusion.91
  329.4 2.8 fusion.91
  335.7 2.9 fusion.91
  342.0 2.9 fusion.91
  346.0 3.0 copy.53
  349.0 4.4 copy.54
  353.4 110.1 %while.33 = (s32[]{:T(128)}, bf16[896,20,128]{2,0,1:T(8,128)(2,1)}, f32[896,20,128]{2,0,1:T(8,128)}, f32[896,20]{0,1:T(8,128)S(1)}, bf16[896,20,128]{2,0,1:T(8,1...) while((s32[]{:T(128)}, bf16[896,20,128]{2,0,1:T(8,128)(2,1)}, ...), condition=%wide.region_7.8_spmd.clone, body=%wide.region_4.7_spmd.clone.sunk | while | flops 241549184 | bytes 6755197 | solution.py:83
  356.1 2.8 fusion.100
  361.6 2.8 fusion.100
  367.1 2.8 fusion.100
  372.6 2.8 fusion.100
  378.1 2.8 fusion.100
  383.6 2.8 fusion.100
  389.1 2.8 fusion.100
  394.6 2.8 fusion.100
  400.2 2.8 fusion.100
  405.7 2.8 fusion.100
  411.2 2.8 fusion.100
  416.7 2.8 fusion.100
  422.2 2.8 fusion.100
  427.7 2.8 fusion.100
  433.2 2.8 fusion.100
  438.7 2.8 fusion.100
  444.2 2.8 fusion.100
  449.7 2.8 fusion.100
  455.2 2.8 fusion.100
  460.7 2.8 fusion.100
  463.6 7.8 %copy.58 = bf16[896,20,128]{2,1,0:T(8,128)(2,1)} copy(bf16[896,20,128]{2,0,1:T(8,128)(2,1)} %get-tuple-element.318) | data formatting | bytes 9175040 | tf_op jit(solution)/shard_map/while | solution.py:83
  471.3 8.7 %all_to_all.65 = bf16[2,448,2560]{2,1,0:T(8,128)(2,1)} reshape(bf16[896,20,128]{2,1,0:T(8,128)(2,1)} %copy.58) | data formatting | bytes 9175040 | tf_op jit(solution)/shard_map/all_to_all | solution.py:120
  480.0 53.6 %all_to_all.73 = bf16[2,448,2560]{2,1,0:T(8,128)(2,1)S(1)} all-to-all(bf16[2,448,2560]{2,1,0:T(8,128)(2,1)} %all_to_all.65), channel_id=1, replica_groups=mesh['stretch'=8,'head'=2,'cfg'=2] {'head'}, dimensions={0} | all-to-all | bytes 9175040 | tf_op jit(solution)/shard_map/all_to_all | solution.py:120
  (275 shorter events, 128.4 us)
Async XLA Ops:
  4.8 58.8 %all-to-all-start.1 = ((bf16[448,2,2560]{2,0,1:T(8,128)(2,1)}), bf16[448,2,2560]{2,0,1:T(8,128)(2,1)}, u32[]{:S(2)}, u32[]{:S(2)}) async-start(bf16[448,2,2560]{2,0,1:T(8,128)(2,1)} %bitcast.86), calls=%async_computation.1 | async-start | bytes 9175040 | tf_op jit(solution)/shard_map/all_to_all | solution.py:101
  63.6 57.1 %all-to-all-start.2 = ((bf16[448,2,2560]{2,0,1:T(8,128)(2,1)}), bf16[448,2,2560]{2,0,1:T(8,128)(2,1)}, u32[]{:S(2)}, u32[]{:S(2)}) async-start(bf16[448,2,2560]{2,0,1:T(8,128)(2,1)} %bitcast.85), calls=%async_computation.2 | async-start | bytes 9175040 | tf_op jit(solution)/shard_map/all_to_all | solution.py:102
  120.6 5.9 %copy-start = (s32[8]{0:T(128)S(1)}, s32[8]{0:T(128)}, u32[]{:S(2)}) copy-start(s32[8]{0:T(128)} %param.12) | copy-start | bytes 100
  120.6 7.1 %copy-start.1 = (s32[8]{0:T(128)S(1)}, s32[8]{0:T(128)}, u32[]{:S(2)}) copy-start(s32[8]{0:T(128)} %param.13) | copy-start | bytes 100
  120.6 56.2 %all-to-all-start = ((bf16[448,2,2560]{2,0,1:T(8,128)(2,1)}), bf16[448,2,2560]{2,0,1:T(8,128)(2,1)}, u32[]{:S(2)}, u32[]{:S(2)}) async-start(bf16[448,2,2560]{2,0,1:T(8,128)(2,1)} %bitcast.84), calls=%async_computation | async-start | bytes 9175040 | tf_op jit(solution)/shard_map/all_to_all | solution.py:100
  131.0 215.1 %collective-permute-start = (bf16[512,2560]{1,0:T(8,128)(2,1)S(1)}, bf16[512,2560]{1,0:T(8,128)(2,1)}, u32[]{:S(2)}, u32[]{:S(2)}) collective-permute-start(bf16[512,2560]{1,0:T(8,128)(2,1)S(1)} %constant_dynamic-slice_fusion.1), channel_id=1, source_target_pairs={{0,4},{4,8},{8,12},{12,16},{16,20},{20,24},{24,28},{1,5},{5,9},{9,... | collective-permute-start | bytes 7864328 | tf_op jit(solution)/shard_map/ppermute | solution.py:19
  139.2 209.8 %collective-permute-start.1 = (bf16[512,2560]{1,0:T(8,128)(2,1)}, bf16[512,2560]{1,0:T(8,128)(2,1)}, u32[]{:S(2)}, u32[]{:S(2)}) collective-permute-start(bf16[512,2560]{1,0:T(8,128)(2,1)} %constant_dynamic-slice_fusion.2), channel_id=1, source_target_pairs={{0,4},{4,8},{8,12},{12,16},{16,20},{20,24},{24,28},{1,5},{5,9},{9,... | collective-permute-start | bytes 7864328 | tf_op jit(solution)/shard_map/ppermute | solution.py:19
where the time goes:
time: 540 us; the launch traced here: 536 us
  matrix products  177 us (33%)
  waiting for transfers between devices  129 us (24%)
  local copies, waits for them, and re-layouts  94.8 us (18%)
  blocking collectives  53.6 us (10%)
  other arithmetic  53.1 us (10%)
  starting transfers between devices  25.7 us (5%)
    dot_general x40, matrix products, head_block(): jnp.dot(weights.astype(jnp.bfloat16), v_head, preferred_element_type=jnp....  114 us
    dot_general x40, matrix products, head_block(): lax.dot_general(q_head, k_head, (((1,), (1,)), ((), ())), preferred_eleme...  62.5 us
    all_to_all x1, blocking collectives, body(): lax.all_to_all(mixed.reshape(span, local), 'head', split_axis=0, concat_a...  53.6 us
    all_to_all x1, waiting for transfers between devices, body(): lax.all_to_all(keys, 'head', split_axis=1, concat_axis=0, tiled=True)  48.3 us
    all_to_all x1, waiting for transfers between devices, body(): lax.all_to_all(values, 'head', split_axis=1, concat_axis=0, tiled=True)  46.5 us
    all_to_all x1, waiting for transfers between devices, body(): lax.all_to_all(queries, 'head', split_axis=1, concat_axis=0, tiled=True)  34.1 us
    reduce_sum x40, other arithmetic, head_block(): total = jnp.sum(weights, axis=1)  26.7 us
    lt x40, other arithmetic, body(): live = spot < count_own  24.9 us
  transfers between devices with their start and end apart: 5, of which 3 were waited for; matrix products, arithmetic and copies ran while one was open for 35% of the time, Pallas kernels for 0%

commit v1 on v0

v1 whole, which is shorter than its diff:
```python
import functools
import math

import jax
import jax.numpy as jnp
from jax import lax
from jax.experimental import pallas as pl
from jax.experimental.pallas import tpu as pltpu
from jax.sharding import PartitionSpec as P

HD = 128
FT = 128
FRAMES = 7
MOT_CAP = 4
NEG = -1e30
MESH = pl.DeviceIdType.MESH

AHEAD = 4
LEAD = 2


def kernel(
    groups, stretches, count, rows, sub,
    frames_ref, motion_ref, q_ref, k_ref, v_ref, out_ref,
    qb, kb, vb, kt, vt, ob, bias,
    in_send, in_recv, in_local, out_send, out_recv, out_local, mot_send, mot_recv,
):
    span = rows * groups
    tail = MOT_CAP * FT
    local = count * HD
    me = lax.axis_index("head")
    stretch = lax.axis_index("stretch")
    after = lax.rem(stretch + 1, stretches)
    before = lax.rem(stretch + stretches - 1, stretches)
    live_frames = frames_ref[stretch]
    motion_frames = motion_ref[stretch]

    def peer(offset):
        return lax.rem(me + offset, groups)

    def rows_of(owner):
        return pl.ds(pl.multiple_of(owner * rows, 16), rows)

    def columns(owner, head):
        return pl.ds(pl.multiple_of(owner * local + head * HD, HD), HD)

    sources = (k_ref, v_ref, q_ref)
    targets = (kb, vb, qb)

    def exchange(which, head, offset, owner):
        to = peer(offset)
        land = me if owner is None else owner
        return pltpu.make_async_remote_copy(
            src_ref=sources[which].at[:, columns(to, head)],
            dst_ref=targets[which].at[head, rows_of(land), :],
            send_sem=in_send.at[which, head, offset - 1],
            recv_sem=in_recv.at[which, head, offset - 1],
            device_id={"head": to},
            device_id_type=MESH,
        )

    def keep(which, head):
        return pltpu.make_async_copy(
            sources[which].at[:, columns(me, head)],
            targets[which].at[head, rows_of(me), :],
            in_local.at[which, head],
        )

    def pass_on(which, head):
        return pltpu.make_async_remote_copy(
            src_ref=(kt, vt)[which].at[head],
            dst_ref=(kb, vb)[which].at[head, pl.ds(span, tail), :],
            send_sem=mot_send.at[which, head],
            recv_sem=mot_recv.at[which, head],
            device_id={"stretch": after},
            device_id_type=MESH,
        )

    def give_back(head, offset, owner):
        to = peer(offset)
        group = me if owner is None else owner
        return pltpu.make_async_remote_copy(
            src_ref=ob.at[head, rows_of(to), :],
            dst_ref=out_ref.at[:, columns(group, head)],
            send_sem=out_send.at[head, offset - 1],
            recv_sem=out_recv.at[head, offset - 1],
            device_id={"head": to},
            device_id_type=MESH,
        )

    def own_output(head):
        return pltpu.make_async_copy(
            ob.at[head, rows_of(me), :],
            out_ref.at[:, columns(me, head)],
            out_local.at[head],
        )

    def start(which, head):
        for offset in range(1, groups):
            exchange(which, head, offset, None).start()
        keep(which, head).start()

    def arrived(which, head):
        keep(which, head).wait()
        for offset in range(1, groups):
            exchange(which, head, offset, peer(groups - offset)).wait_recv()

    def slot(index):
        @pl.when(index < count)
        def _():
            start(0, index)
            start(1, index)

        @pl.when(jnp.logical_and(index >= 1, index <= count))
        def _():
            start(2, index - 1)

    def forward(head):
        for which, (buffer, ready) in enumerate(((kb, kt), (vb, vt))):
            arrived(which, head)
            for block in range(MOT_CAP):
                chosen = buffer[head, pl.ds(block * FT, FT), :].astype(jnp.float32)
                for skip in range(1, FRAMES - MOT_CAP + 1):
                    other = buffer[head, pl.ds((block + skip) * FT, FT), :].astype(jnp.float32)
                    chosen = jnp.where(live_frames == MOT_CAP + skip, other, chosen)
                ready[head, pl.ds(block * FT, FT), :] = chosen.astype(jnp.bfloat16)
            pass_on(which, head).start()

    scale = math.log2(math.e) / math.sqrt(HD)

    def attend(head, base):
        scores = lax.dot_general(
            qb[head, pl.ds(base, sub), :], kb[head],
            (((1,), (1,)), ((), ())), preferred_element_type=jnp.float32,
        )
        scores = scores * scale + bias[...]
        top = jnp.max(scores, axis=1, keepdims=True)
        weights = jnp.exp2(scores - top)
        total = jnp.sum(weights, axis=1, keepdims=True)
        acc = jnp.dot(weights.astype(jnp.bfloat16), vb[head], preferred_element_type=jnp.float32)
        row = base + lax.broadcasted_iota(jnp.int32, (sub, 1), 0)
        mixed = jnp.where(row < live_frames * FT, acc / total, 0.0)
        ob[head, pl.ds(base, sub), :] = mixed.astype(jnp.bfloat16)

    barrier = pltpu.get_barrier_semaphore()
    for offset in range(1, groups):
        pl.semaphore_signal(barrier, inc=1, device_id={"head": peer(offset)}, device_id_type=MESH)
    for other in (after, before):
        pl.semaphore_signal(barrier, inc=1, device_id={"stretch": other}, device_id_type=MESH)
    pl.semaphore_wait(barrier, groups + 1)

    for index in range(AHEAD):
        slot(jnp.int32(index))

    spot = lax.broadcasted_iota(jnp.int32, (1, span + tail), 1)
    own = jnp.logical_and(spot < span, spot < live_frames * FT)
    mot = spot >= span + (MOT_CAP - motion_frames) * FT
    bias[...] = jnp.where(jnp.logical_or(own, mot), 0.0, NEG)

    for head in range(LEAD):
        forward(jnp.int32(head))

    def step(head, carry):
        slot(head + AHEAD)

        @pl.when(head + LEAD < count)
        def _():
            forward(head + LEAD)

        arrived(2, head)
        for which in range(2):
            pass_on(which, head).wait_recv()
        for offset in range(1, groups + 1):
            owner = peer(offset)

            def block(index, c):
                attend(head, pl.multiple_of(owner * rows + index * sub, 16))
                return c

            lax.fori_loop(0, rows // sub, block, 0)
            if offset < groups:
                give_back(head, offset, None).start()
            else:
                own_output(head).start()
        return carry

    lax.fori_loop(0, count, step, 0)

    def drain(head, carry):
        for which in range(3):
            for offset in range(1, groups):
                exchange(which, head, offset, None).wait_send()
        for which in range(2):
            pass_on(which, head).wait_send()
        for offset in range(1, groups):
            give_back(head, offset, None).wait_send()
            give_back(head, offset, peer(groups - offset)).wait_recv()
        own_output(head).wait()
        return carry

    lax.fori_loop(0, count, drain, 0)


def body(groups, stretches, queries, keys, values, frames, motion):
    rows, width = queries.shape
    span = rows * groups
    tail = MOT_CAP * FT
    local = width // groups
    count = local // HD
    sub = rows // 2 if rows > 256 else rows
    wide = jnp.bfloat16
    dma = pltpu.SemaphoreType.DMA
    return pl.pallas_call(
        functools.partial(kernel, groups, stretches, count, rows, sub),
        out_shape=jax.ShapeDtypeStruct((rows, width), wide),
        in_specs=[pl.BlockSpec(memory_space=pltpu.SMEM)] * 2
        + [pl.BlockSpec(memory_space=pltpu.HBM)] * 3,
        out_specs=pl.BlockSpec(memory_space=pltpu.HBM),
        scratch_shapes=[
            pltpu.VMEM((count, span, HD), wide),
            pltpu.VMEM((count, span + tail, HD), wide),
            pltpu.VMEM((count, span + tail, HD), wide),
            pltpu.VMEM((count, tail, HD), wide),
            pltpu.VMEM((count, tail, HD), wide),
            pltpu.VMEM((count, span, HD), wide),
            pltpu.VMEM((1, span + tail), jnp.float32),
            dma((3, count, groups - 1)),
            dma((3, count, groups - 1)),
            dma((3, count)),
            dma((count, groups - 1)),
            dma((count, groups - 1)),
            dma((count,)),
            dma((2, count)),
            dma((2, count)),
        ],
        compiler_params=pltpu.CompilerParams(
            collective_id=0, has_side_effects=True, vmem_limit_bytes=56 * 1024 * 1024
        ),
        cost_estimate=pl.CostEstimate(
            flops=4 * span * (span + tail) * local,
            bytes_accessed=8 * rows * width,
            transcendentals=span * (span + tail) * count,
        ),
    )(frames, motion, queries, keys, values)


def solution(mesh):
    placed = P(("cfg", "stretch", "head"), None)
    return jax.shard_map(
        functools.partial(body, mesh.shape["head"], mesh.shape["stretch"]),
        mesh=mesh,
        in_specs=(placed, placed, placed, P(), P()),
        out_specs=placed,
        check_vma=False,
    )
```

time: 540 us -> 213 us (0.39)
  Pallas kernels: 0 us -> 208 us
  matrix products: 177 us -> 0 us
  waiting for transfers between devices: 129 us -> 0 us
  local copies, waits for them, and re-layouts: 94.8 us -> 4.74 us
  blocking collectives: 53.6 us -> 0 us
  other arithmetic: 53.1 us -> 0 us
  starting transfers between devices: 25.7 us -> 0 us
    pallas_call x0 -> x1, Pallas kernels: none -> 208 us  [body(): pl.pallas_call(functools.partial(kernel, groups, stretches, count, rows,...]
    dot_general x80 -> x0, matrix products: 177 us -> none  [the longest x40 114 us: head_block(): jnp.dot(weights.astype(jnp.bfloat16), v_head, preferred_element_type=jnp....]
    all_to_all x3 -> x0, waiting for transfers between devices: 129 us -> none  [the longest x1 48.3 us: body(): lax.all_to_all(keys, 'head', split_axis=1, concat_axis=0, tiled=True)]
    all_to_all x1 -> x0, blocking collectives: 53.6 us -> none  [body(): lax.all_to_all(mixed.reshape(span, local), 'head', split_axis=0, concat_a...]
    reduce_sum x40 -> x0, other arithmetic: 26.7 us -> none  [head_block(): total = jnp.sum(weights, axis=1)]
    reshape x3 -> x0, local copies, waits for them, and re-layouts: 26.2 us -> none  [the longest x1 8.75 us: body(): q_shaped = q_heads.reshape(span, count, HD)]
    all_to_all x5 -> x0, local copies, waits for them, and re-layouts: 25.7 us -> none  [the longest x2 11.4 us: body(): lax.all_to_all(mixed.reshape(span, local), 'head', split_axis=0, concat_a...]
    lt x40 -> x0, other arithmetic: 24.9 us -> none  [body(): live = spot < count_own]
  transfers between devices with their start and end apart: 5 -> 0, of which waited for: 3 -> 0; matrix products, arithmetic and copies ran while one was open for 35% -> 0% of each run, Pallas kernels for 0% -> 0%
where the time goes in v1:
time: 213 us
  Pallas kernels  208 us (98%)
  local copies, waits for them, and re-layouts  4.74 us (2%)
    pallas_call x1, Pallas kernels, body(): pl.pallas_call(functools.partial(kernel, groups, stretches, count, rows,...  208 us
    unnamed x1, local copies, waits for them, and re-layouts  4.74 us

profile of v1, /device:TPU:0, one launch (start us, length us, event | category | flops | bytes accessed | tf_op | source)
XLA Modules:
  0.0 213.1 jit_solution(17888961955586699607)
XLA Ops:
  0.0 208.4 %shard_map.55 = bf16[448,5120]{1,0:T(8,128)(2,1)} custom-call(s32[8]{0:T(128)} %frames_ref.1, s32[8]{0:T(128)} %motion_ref.1, bf16[448,5120]{1,0:T(8,128)(2,1)} %q_ref.1, bf16[448,5120]{1,0:T(8,128)(2,1)} %k_ref.1, bf16[448,5120]{1,0:T(8,128)(2,1)} %v_ref.1), custom_call_target="tpu_custom_call" | custom-call | flops 12918456320 | bytes 18350080 | tf_op jit(solution)/shard_map/pallas_call | solution.py:213
  208.4 4.7 %copy.7 = bf16[448,5120]{1,0:T(8,128)(2,1)} copy(bf16[448,5120]{1,0:T(8,128)(2,1)} %shard_map.55) | data formatting | bytes 9175040

commit v2 on v1

--- a/solution.py
+++ b/solution.py
@@ -23,15 +23,18 @@
     groups, stretches, count, rows, sub,
     frames_ref, motion_ref, q_ref, k_ref, v_ref, out_ref,
     qb, kb, vb, kt, vt, ob, bias,
-    in_send, in_recv, in_local, out_send, out_recv, out_local, mot_send, mot_recv,
+    in_send, in_recv, in_local, q_send, q_recv, out_send, out_recv, out_local, mot_send, mot_recv,
 ):
     span = rows * groups
     tail = MOT_CAP * FT
     local = count * HD
     me = lax.axis_index("head")
     stretch = lax.axis_index("stretch")
-    after = lax.rem(stretch + 1, stretches)
-    before = lax.rem(stretch + stretches - 1, stretches)
+    has_after = stretch < stretches - 1
+    has_before = stretch > 0
+    after = jnp.minimum(stretch + 1, stretches - 1)
+    before = jnp.maximum(stretch - 1, 0)
+    chunks = rows // sub
     live_frames = frames_ref[stretch]
     motion_frames = motion_ref[stretch]
 
@@ -43,6 +46,9 @@
 
     def columns(owner, head):
         return pl.ds(pl.multiple_of(owner * local + head * HD, HD), HD)
+
+    def chunk_of(owner, chunk):
+        return pl.ds(pl.multiple_of(owner * rows + chunk * sub, 16), sub)
 
     sources = (k_ref, v_ref, q_ref)
     targets = (kb, vb, qb)
@@ -59,6 +65,18 @@
             device_id_type=MESH,
         )
 
+    def query(head, offset, chunk, owner):
+        to = peer(offset)
+        land = me if owner is None else owner
+        return pltpu.make_async_remote_copy(
+            src_ref=q_ref.at[pl.ds(pl.multiple_of(chunk * sub, 16), sub), columns(to, head)],
+            dst_ref=qb.at[head, chunk_of(land, chunk), :],
+            send_sem=q_send.at[head, offset - 1, chunk],
+            recv_sem=q_recv.at[head, offset - 1, chunk],
+            device_id={"head": to},
+            device_id_type=MESH,
+        )
+
     def keep(which, head):
         return pltpu.make_async_copy(
             sources[which].at[:, columns(me, head)],
@@ -76,14 +94,14 @@
             device_id_type=MESH,
         )
 
-    def give_back(head, offset, owner):
+    def give_back(head, offset, chunk, owner):
         to = peer(offset)
         group = me if owner is None else owner
         return pltpu.make_async_remote_copy(
-            src_ref=ob.at[head, rows_of(to), :],
-            dst_ref=out_ref.at[:, columns(group, head)],
-            send_sem=out_send.at[head, offset - 1],
-            recv_sem=out_recv.at[head, offset - 1],
+            src_ref=ob.at[head, chunk_of(to, chunk), :],
+            dst_ref=out_ref.at[pl.ds(pl.multiple_of(chunk * sub, 16), sub), columns(group, head)],
+            send_sem=out_send.at[head, offset - 1, chunk],
+            recv_sem=out_recv.at[head, offset - 1, chunk],
             device_id={"head": to},
             device_id_type=MESH,
         )
@@ -111,9 +129,12 @@
             start(0, index)
             start(1, index)
 
-        @pl.when(jnp.logical_and(index >= 1, index <= count))
-        def _():
-            start(2, index - 1)
+        @pl.when(jnp.logical_and(index >= LEAD, index < count + LEAD))
+        def _():
+            for chunk in range(chunks):
+                for offset in range(1, groups):
+                    query(index - LEAD, offset, chunk, None).start()
+            keep(2, index - LEAD).start()
 
     def forward(head):
         for which, (buffer, ready) in enumerate(((kb, kt), (vb, vt))):
@@ -124,7 +145,10 @@
                     other = buffer[head, pl.ds((block + skip) * FT, FT), :].astype(jnp.float32)
                     chosen = jnp.where(live_frames == MOT_CAP + skip, other, chosen)
                 ready[head, pl.ds(block * FT, FT), :] = chosen.astype(jnp.bfloat16)
-            pass_on(which, head).start()
+
+            @pl.when(has_after)
+            def _():
+                pass_on(which, head).start()
 
     scale = math.log2(math.e) / math.sqrt(HD)
 
@@ -145,9 +169,15 @@
     barrier = pltpu.get_barrier_semaphore()
     for offset in range(1, groups):
         pl.semaphore_signal(barrier, inc=1, device_id={"head": peer(offset)}, device_id_type=MESH)
-    for other in (after, before):
-        pl.semaphore_signal(barrier, inc=1, device_id={"stretch": other}, device_id_type=MESH)
-    pl.semaphore_wait(barrier, groups + 1)
+    for other, there in ((after, has_after), (before, has_before)):
+
+        @pl.when(there)
+        def _():
+            pl.semaphore_signal(barrier, inc=1, device_id={"stretch": other}, device_id_type=MESH)
+
+    pl.semaphore_wait(
+        barrier, groups - 1 + has_after.astype(jnp.int32) + has_before.astype(jnp.int32)
+    )
 
     for index in range(AHEAD):
         slot(jnp.int32(index))
@@ -157,6 +187,15 @@
     mot = spot >= span + (MOT_CAP - motion_frames) * FT
     bias[...] = jnp.where(jnp.logical_or(own, mot), 0.0, NEG)
 
+    @pl.when(jnp.logical_not(has_before))
+    def _():
+        def clear(head, carry):
+            for buffer in (kb, vb):
+                buffer[head, pl.ds(span, tail), :] = jnp.zeros((tail, HD), jnp.bfloat16)
+            return carry
+
+        lax.fori_loop(0, count, clear, 0)
+
     for head in range(LEAD):
         forward(jnp.int32(head))
 
@@ -167,34 +206,47 @@
         def _():
             forward(head + LEAD)
 
-        arrived(2, head)
-        for which in range(2):
-            pass_on(which, head).wait_recv()
-        for offset in range(1, groups + 1):
-            owner = peer(offset)
-
-            def block(index, c):
-                attend(head, pl.multiple_of(owner * rows + index * sub, 16))
+        @pl.when(has_before)
+        def _():
+            for which in range(2):
+                pass_on(which, head).wait_recv()
+
+        for offset in range(1, groups):
+            to = peer(offset)
+
+            def block(chunk, c):
+                query(head, groups - offset, chunk, to).wait_recv()
+                attend(head, pl.multiple_of(to * rows + chunk * sub, 16))
+                give_back(head, offset, chunk, None).start()
                 return c
 
-            lax.fori_loop(0, rows // sub, block, 0)
-            if offset < groups:
-                give_back(head, offset, None).start()
-            else:
-                own_output(head).start()
+            lax.fori_loop(0, chunks, block, 0)
+        keep(2, head).wait()
+
+        def own_block(chunk, c):
+            attend(head, pl.multiple_of(me * rows + chunk * sub, 16))
+            return c
+
+        lax.fori_loop(0, chunks, own_block, 0)
+        own_output(head).start()
         return carry
 
     lax.fori_loop(0, count, step, 0)
 
     def drain(head, carry):
-        for which in range(3):
-            for offset in range(1, groups):
+        for offset in range(1, groups):
+            for which in range(2):
                 exchange(which, head, offset, None).wait_send()
-        for which in range(2):
-            pass_on(which, head).wait_send()
-        for offset in range(1, groups):
-            give_back(head, offset, None).wait_send()
-            give_back(head, offset, peer(groups - offset)).wait_recv()
+            for chunk in range(chunks):
+                query(head, offset, chunk, None).wait_send()
+                give_back(head, offset, chunk, None).wait_send()
+                give_back(head, offset, chunk, peer(groups - offset)).wait_recv()
+
+        @pl.when(has_after)
+        def _():
+            for which in range(2):
+                pass_on(which, head).wait_send()
+
         own_output(head).wait()
         return carry
 
@@ -207,15 +259,16 @@
     tail = MOT_CAP * FT
     local = width // groups
     count = local // HD
-    sub = rows // 2 if rows > 256 else rows
+    sub = rows // 4 if rows > 256 else rows
+    chunks = rows // sub
     wide = jnp.bfloat16
     dma = pltpu.SemaphoreType.DMA
     return pl.pallas_call(
         functools.partial(kernel, groups, stretches, count, rows, sub),
-        out_shape=jax.ShapeDtypeStruct((rows, width), wide),
+        out_shape=pltpu.VMEM((rows, width), wide),
         in_specs=[pl.BlockSpec(memory_space=pltpu.SMEM)] * 2
         + [pl.BlockSpec(memory_space=pltpu.HBM)] * 3,
-        out_specs=pl.BlockSpec(memory_space=pltpu.HBM),
+        out_specs=pl.BlockSpec(memory_space=pltpu.VMEM),
         scratch_shapes=[
             pltpu.VMEM((count, span, HD), wide),
             pltpu.VMEM((count, span + tail, HD), wide),
@@ -224,17 +277,19 @@
             pltpu.VMEM((count, tail, HD), wide),
             pltpu.VMEM((count, span, HD), wide),
             pltpu.VMEM((1, span + tail), jnp.float32),
-            dma((3, count, groups - 1)),
-            dma((3, count, groups - 1)),
+            dma((2, count, groups - 1)),
+            dma((2, count, groups - 1)),
             dma((3, count)),
-            dma((count, groups - 1)),
-            dma((count, groups - 1)),
+            dma((count, groups - 1, chunks)),
+            dma((count, groups - 1, chunks)),
+            dma((count, groups - 1, chunks)),
+            dma((count, groups - 1, chunks)),
             dma((count,)),
             dma((2, count)),
             dma((2, count)),
         ],
         compiler_params=pltpu.CompilerParams(
-            collective_id=0, has_side_effects=True, vmem_limit_bytes=56 * 1024 * 1024
+            collective_id=0, has_side_effects=True, vmem_limit_bytes=48 * 1024 * 1024
         ),
         cost_estimate=pl.CostEstimate(
             flops=4 * span * (span + tail) * local,

time: 213 us -> 211 us (level)
    unnamed x1 -> x5, local copies, waits for them, and re-layouts: 4.74 us -> 3.45 us
where the time goes in v2:
time: 211 us
  Pallas kernels  207 us (98%)
  local copies, waits for them, and re-layouts  3.45 us (2%)
    pallas_call x1, Pallas kernels, body(): pl.pallas_call(functools.partial(kernel, groups, stretches, count, rows,...  207 us

profile of v2, /device:TPU:0, one launch (start us, length us, event | category | flops | bytes accessed | tf_op | source)
XLA Modules:
  0.0 210.7 jit_solution(8070008006851277133)
XLA Ops:
  0.0 0.0 copy-start
  0.0 0.7 copy-done
  0.7 0.0 copy-start.1
  0.7 0.7 copy-done.1
  1.3 207.3 %shard_map.55 = bf16[448,5120]{1,0:T(8,128)(2,1)S(1)} custom-call(s32[8]{0:T(128)S(1)} %copy-done, s32[8]{0:T(128)S(1)} %copy-done.1, bf16[448,5120]{1,0:T(8,128)(2,1)} %q_ref.1, bf16[448,5120]{1,0:T(8,128)(2,1)} %k_ref.1, bf16[448,5120]{1,0:T(8,128)(2,1)} %v_ref.1), custom_call_target="tpu_custom_call" | custom-call | flops 12918456320 | bytes 18350080 | tf_op jit(solution)/shard_map/pallas_call | solution.py:266
  208.6 2.1 %copy.7 = bf16[448,5120]{1,0:T(8,128)(2,1)} copy(bf16[448,5120]{1,0:T(8,128)(2,1)S(1)} %shard_map.55) | data formatting | bytes 9175040
Async XLA Ops:
  0.0 0.7 copy-start
  0.7 0.7 copy-start.1

commit v3 on v2

--- a/solution.py
+++ b/solution.py
@@ -16,6 +16,7 @@
 MESH = pl.DeviceIdType.MESH
 
 AHEAD = 4
+LAG = 3
 LEAD = 2
 
 
@@ -199,41 +200,7 @@
     for head in range(LEAD):
         forward(jnp.int32(head))
 
-    def step(head, carry):
-        slot(head + AHEAD)
-
-        @pl.when(head + LEAD < count)
-        def _():
-            forward(head + LEAD)
-
-        @pl.when(has_before)
-        def _():
-            for which in range(2):
-                pass_on(which, head).wait_recv()
-
-        for offset in range(1, groups):
-            to = peer(offset)
-
-            def block(chunk, c):
-                query(head, groups - offset, chunk, to).wait_recv()
-                attend(head, pl.multiple_of(to * rows + chunk * sub, 16))
-                give_back(head, offset, chunk, None).start()
-                return c
-
-            lax.fori_loop(0, chunks, block, 0)
-        keep(2, head).wait()
-
-        def own_block(chunk, c):
-            attend(head, pl.multiple_of(me * rows + chunk * sub, 16))
-            return c
-
-        lax.fori_loop(0, chunks, own_block, 0)
-        own_output(head).start()
-        return carry
-
-    lax.fori_loop(0, count, step, 0)
-
-    def drain(head, carry):
+    def drain(head):
         for offset in range(1, groups):
             for which in range(2):
                 exchange(which, head, offset, None).wait_send()
@@ -248,9 +215,51 @@
                 pass_on(which, head).wait_send()
 
         own_output(head).wait()
+
+    def step(head, carry):
+        slot(head + AHEAD)
+
+        @pl.when(head + LEAD < count)
+        def _():
+            forward(head + LEAD)
+
+        @pl.when(has_before)
+        def _():
+            for which in range(2):
+                pass_on(which, head).wait_recv()
+
+        for offset in range(1, groups):
+            to = peer(offset)
+
+            def block(chunk, c):
+                query(head, groups - offset, chunk, to).wait_recv()
+                attend(head, pl.multiple_of(to * rows + chunk * sub, 16))
+                give_back(head, offset, chunk, None).start()
+                return c
+
+            lax.fori_loop(0, chunks, block, 0)
+        keep(2, head).wait()
+
+        def own_block(chunk, c):
+            attend(head, pl.multiple_of(me * rows + chunk * sub, 16))
+            return c
+
+        lax.fori_loop(0, chunks, own_block, 0)
+        own_output(head).start()
+
+        @pl.when(head >= LAG)
+        def _():
+            drain(head - LAG)
+
         return carry
 
-    lax.fori_loop(0, count, drain, 0)
+    lax.fori_loop(0, count, step, 0)
+
+    def last(head, carry):
+        drain(head)
+        return carry
+
+    lax.fori_loop(max(count - LAG, 0), count, last, 0)
 
 
 def body(groups, stretches, queries, keys, values, frames, motion):
@@ -289,7 +298,7 @@
             dma((2, count)),
         ],
         compiler_params=pltpu.CompilerParams(
-            collective_id=0, has_side_effects=True, vmem_limit_bytes=48 * 1024 * 1024
+            collective_id=0, has_side_effects=True, vmem_limit_bytes=58 * 1024 * 1024
         ),
         cost_estimate=pl.CostEstimate(
             flops=4 * span * (span + tail) * local,

time: 211 us -> 210 us (level)
  no operation moved by 1% of the time
where the time goes in v3:
time: 210 us
  Pallas kernels  207 us (99%)
  local copies, waits for them, and re-layouts  2.15 us (1%)
    pallas_call x1, Pallas kernels, body(): pl.pallas_call(functools.partial(kernel, groups, stretches, count, rows,...  207 us

profile of v3, /device:TPU:0, one launch (start us, length us, event | category | flops | bytes accessed | tf_op | source)
XLA Modules:
  0.0 209.6 jit_solution(3491716381510085888)
XLA Ops:
  0.0 207.4 %shard_map.55 = bf16[448,5120]{1,0:T(8,128)(2,1)S(1)} custom-call(s32[8]{0:T(128)} %frames_ref.1, s32[8]{0:T(128)} %motion_ref.1, bf16[448,5120]{1,0:T(8,128)(2,1)} %q_ref.1, bf16[448,5120]{1,0:T(8,128)(2,1)} %k_ref.1, bf16[448,5120]{1,0:T(8,128)(2,1)} %v_ref.1), custom_call_target="tpu_custom_call" | custom-call | flops 12918456320 | bytes 18350080 | tf_op jit(solution)/shard_map/pallas_call | solution.py:275
  207.4 2.1 %copy.7 = bf16[448,5120]{1,0:T(8,128)(2,1)} copy(bf16[448,5120]{1,0:T(8,128)(2,1)S(1)} %shard_map.55) | data formatting | bytes 9175040

commit v4 on v2

v4 whole, which is shorter than its diff:
```python
import functools
import math

import jax
import jax.numpy as jnp
from jax import lax
from jax.experimental import pallas as pl
from jax.experimental.pallas import tpu as pltpu
from jax.sharding import PartitionSpec as P

HD = 128
FT = 128
FRAMES = 7
MOT_CAP = 4
NEG = -1e30
MESH = pl.DeviceIdType.MESH

PACK = 2
AHEAD = 3
LEAD = 1
LAG = 2


def kernel(
    groups, stretches, count, pack, rows, sub,
    frames_ref, motion_ref, q_ref, k_ref, v_ref, out_ref,
    qb, kb, vb, kt, vt, ob, bias,
    in_send, in_recv, in_local, q_send, q_recv, out_send, out_recv, out_local, mot_send, mot_recv,
):
    span = rows * groups
    tail = MOT_CAP * FT
    unit = pack * HD
    local = count * unit
    fine = rows // sub
    me = lax.axis_index("head")
    stretch = lax.axis_index("stretch")
    has_after = stretch < stretches - 1
    has_before = stretch > 0
    after = jnp.minimum(stretch + 1, stretches - 1)
    before = jnp.maximum(stretch - 1, 0)
    live_frames = frames_ref[stretch]
    motion_frames = motion_ref[stretch]

    def peer(offset):
        return lax.rem(me + offset, groups)

    def columns(owner, index):
        return pl.ds(pl.multiple_of(owner * local + index * unit, unit), unit)

    def part_rows(base, part, parts):
        size = rows // parts
        return pl.ds(pl.multiple_of(base + part * size, 16), size)

    sources = (k_ref, v_ref, q_ref)
    targets = (kb, vb, qb)

    def exchange(which, index, offset, owner):
        to = peer(offset)
        land = me if owner is None else owner
        return pltpu.make_async_remote_copy(
            src_ref=sources[which].at[:, columns(to, index)],
            dst_ref=targets[which].at[index, part_rows(land * rows, 0, 1), :],
            send_sem=in_send.at[which, index, offset - 1],
            recv_sem=in_recv.at[which, index, offset - 1],
            device_id={"head": to},
            device_id_type=MESH,
        )

    def query(index, offset, owner, part, parts):
        to = peer(offset)
        land = me if owner is None else owner
        return pltpu.make_async_remote_copy(
            src_ref=q_ref.at[part_rows(0, part, parts), columns(to, index)],
            dst_ref=qb.at[index, part_rows(land * rows, part, parts), :],
            send_sem=q_send.at[index, offset - 1, part],
            recv_sem=q_recv.at[index, offset - 1, part],
            device_id={"head": to},
            device_id_type=MESH,
        )

    def keep(which, index):
        return pltpu.make_async_copy(
            sources[which].at[:, columns(me, index)],
            targets[which].at[index, part_rows(me * rows, 0, 1), :],
            in_local.at[which, index],
        )

    def pass_on(which, index):
        return pltpu.make_async_remote_copy(
            src_ref=(kt, vt)[which].at[index],
            dst_ref=(kb, vb)[which].at[index, pl.ds(span, tail), :],
            send_sem=mot_send.at[which, index],
            recv_sem=mot_recv.at[which, index],
            device_id={"stretch": after},
            device_id_type=MESH,
        )

    def give_back(index, offset, owner, part, parts):
        to = peer(offset)
        group = me if owner is None else owner
        return pltpu.make_async_remote_copy(
            src_ref=ob.at[index, part_rows(to * rows, part, parts), :],
            dst_ref=out_ref.at[part_rows(0, part, parts), columns(group, index)],
            send_sem=out_send.at[index, offset - 1, part],
            recv_sem=out_recv.at[index, offset - 1, part],
            device_id={"head": to},
            device_id_type=MESH,
        )

    def own_output(index):
        return pltpu.make_async_copy(
            ob.at[index, part_rows(me * rows, 0, 1), :],
            out_ref.at[:, columns(me, index)],
            out_local.at[index],
        )

    def send_queries(index, parts):
        for part in range(parts):
            for offset in range(1, groups):
                query(index, offset, None, part, parts).start()
        keep(2, index).start()

    def slot(index):
        @pl.when(index < count)
        def _():
            for which in range(2):
                for offset in range(1, groups):
                    exchange(which, index, offset, None).start()
                keep(which, index).start()

        @pl.when(jnp.logical_and(index >= LEAD, index < count + LEAD - 1))
        def _():
            send_queries(index - LEAD, 1)

        @pl.when(index == count + LEAD - 1)
        def _():
            send_queries(count - 1, fine)

    def forward(index):
        for which, (buffer, ready) in enumerate(((kb, kt), (vb, vt))):
            keep(which, index).wait()
            for offset in range(1, groups):
                exchange(which, index, offset, peer(groups - offset)).wait_recv()
            for block in range(MOT_CAP):
                chosen = buffer[index, pl.ds(block * FT, FT), :].astype(jnp.float32)
                for skip in range(1, FRAMES - MOT_CAP + 1):
                    other = buffer[index, pl.ds((block + skip) * FT, FT), :].astype(jnp.float32)
                    chosen = jnp.where(live_frames == MOT_CAP + skip, other, chosen)
                ready[index, pl.ds(block * FT, FT), :] = chosen.astype(jnp.bfloat16)

            @pl.when(has_after)
            def _():
                pass_on(which, index).start()

    scale = math.log2(math.e) / math.sqrt(HD)

    def attend(index, base):
        row = base + lax.broadcasted_iota(jnp.int32, (sub, 1), 0)
        for head in range(pack):
            lanes = slice(head * HD, (head + 1) * HD)
            scores = lax.dot_general(
                qb[index, pl.ds(base, sub), lanes], kb[index, :, lanes],
                (((1,), (1,)), ((), ())), preferred_element_type=jnp.float32,
            )
            scores = scores * scale + bias[...]
            top = jnp.max(scores, axis=1, keepdims=True)
            weights = jnp.exp2(scores - top)
            total = jnp.sum(weights, axis=1, keepdims=True)
            acc = jnp.dot(
                weights.astype(jnp.bfloat16), vb[index, :, lanes],
                preferred_element_type=jnp.float32,
            )
            mixed = jnp.where(row < live_frames * FT, acc / total, 0.0)
            ob[index, pl.ds(base, sub), lanes] = mixed.astype(jnp.bfloat16)

    def attend_rows(index, begin, number):
        def block(step, carry):
            attend(index, pl.multiple_of(begin + step * sub, 16))
            return carry

        lax.fori_loop(0, number, block, 0)

    barrier = pltpu.get_barrier_semaphore()
    for offset in range(1, groups):
        pl.semaphore_signal(barrier, inc=1, device_id={"head": peer(offset)}, device_id_type=MESH)
    for other, there in ((after, has_after), (before, has_before)):

        @pl.when(there)
        def _():
            pl.semaphore_signal(barrier, inc=1, device_id={"stretch": other}, device_id_type=MESH)

    pl.semaphore_wait(
        barrier, groups - 1 + has_after.astype(jnp.int32) + has_before.astype(jnp.int32)
    )

    for index in range(AHEAD):
        slot(jnp.int32(index))

    spot = lax.broadcasted_iota(jnp.int32, (1, span + tail), 1)
    own = jnp.logical_and(spot < span, spot < live_frames * FT)
    mot = spot >= span + (MOT_CAP - motion_frames) * FT
    bias[...] = jnp.where(jnp.logical_or(own, mot), 0.0, NEG)

    @pl.when(jnp.logical_not(has_before))
    def _():
        def clear(index, carry):
            for buffer in (kb, vb):
                buffer[index, pl.ds(span, tail), :] = jnp.zeros((tail, unit), jnp.bfloat16)
            return carry

        lax.fori_loop(0, count, clear, 0)

    for index in range(LEAD):
        forward(jnp.int32(index))

    def work(index, parts):
        slot(index + AHEAD)

        @pl.when(index + LEAD < count)
        def _():
            forward(index + LEAD)

        @pl.when(has_before)
        def _():
            for which in range(2):
                pass_on(which, index).wait_recv()

        keep(2, index).wait()
        attend_rows(index, me * rows, fine)
        own_output(index).start()
        for offset in range(1, groups):
            to = peer(offset)

            def chunk(part, carry):
                query(index, groups - offset, to, part, parts).wait_recv()
                attend_rows(index, to * rows + part * (rows // parts), fine // parts)
                give_back(index, offset, None, part, parts).start()
                return carry

            lax.fori_loop(0, parts, chunk, 0)

    def retire(index, parts):
        for offset in range(1, groups):
            for which in range(2):
                exchange(which, index, offset, None).wait_send()
            for part in range(parts):
                query(index, offset, None, part, parts).wait_send()
                give_back(index, offset, None, part, parts).wait_send()
                give_back(index, offset, peer(groups - offset), part, parts).wait_recv()

        @pl.when(has_after)
        def _():
            for which in range(2):
                pass_on(which, index).wait_send()

        own_output(index).wait()

    def step(index, carry):
        work(index, 1)

        @pl.when(index >= LAG)
        def _():
            retire(index - LAG, 1)

        return carry

    lax.fori_loop(0, count - 1, step, 0)
    work(jnp.int32(count - 1), fine)
    for index in range(max(count - 1 - LAG, 0), count - 1):
        retire(jnp.int32(index), 1)
    retire(jnp.int32(count - 1), fine)


def body(groups, stretches, queries, keys, values, frames, motion):
    rows, width = queries.shape
    span = rows * groups
    tail = MOT_CAP * FT
    local = width // groups
    heads = local // HD
    pack = math.gcd(heads, PACK)
    count = heads // pack
    unit = pack * HD
    sub = rows // 4 if rows % 64 == 0 else rows
    fine = rows // sub
    wide = jnp.bfloat16
    dma = pltpu.SemaphoreType.DMA
    return pl.pallas_call(
        functools.partial(kernel, groups, stretches, count, pack, rows, sub),
        out_shape=pltpu.VMEM((rows, width), wide),
        in_specs=[pl.BlockSpec(memory_space=pltpu.SMEM)] * 2
        + [pl.BlockSpec(memory_space=pltpu.HBM)] * 3,
        out_specs=pl.BlockSpec(memory_space=pltpu.VMEM),
        scratch_shapes=[
            pltpu.VMEM((count, span, unit), wide),
            pltpu.VMEM((count, span + tail, unit), wide),
            pltpu.VMEM((count, span + tail, unit), wide),
            pltpu.VMEM((count, tail, unit), wide),
            pltpu.VMEM((count, tail, unit), wide),
            pltpu.VMEM((count, span, unit), wide),
            pltpu.VMEM((1, span + tail), jnp.float32),
            dma((2, count, groups - 1)),
            dma((2, count, groups - 1)),
            dma((3, count)),
            dma((count, groups - 1, fine)),
            dma((count, groups - 1, fine)),
            dma((count, groups - 1, fine)),
            dma((count, groups - 1, fine)),
            dma((count,)),
            dma((2, count)),
            dma((2, count)),
        ],
        compiler_params=pltpu.CompilerParams(
            collective_id=0, has_side_effects=True, vmem_limit_bytes=58 * 1024 * 1024
        ),
        cost_estimate=pl.CostEstimate(
            flops=4 * span * (span + tail) * local,
            bytes_accessed=8 * rows * width,
            transcendentals=span * (span + tail) * heads,
        ),
    )(frames, motion, queries, keys, values)


def solution(mesh):
    placed = P(("cfg", "stretch", "head"), None)
    return jax.shard_map(
        functools.partial(body, mesh.shape["head"], mesh.shape["stretch"]),
        mesh=mesh,
        in_specs=(placed, placed, placed, P(), P()),
        out_specs=placed,
        check_vma=False,
    )
```

time: 211 us -> 207 us (0.981)
    pallas_call x1, Pallas kernels: 207 us -> 205 us  [body(): pl.pallas_call(functools.partial(kernel, groups, stretches, count, pack,...]
where the time goes in v4:
time: 207 us
  Pallas kernels  205 us (99%)
  local copies, waits for them, and re-layouts  2.15 us (1%)
    pallas_call x1, Pallas kernels, body(): pl.pallas_call(functools.partial(kernel, groups, stretches, count, pack,...  205 us

profile of v4, /device:TPU:0, one launch (start us, length us, event | category | flops | bytes accessed | tf_op | source)
XLA Modules:
  0.0 207.1 jit_solution(8400332583420170760)
XLA Ops:
  0.0 204.9 %shard_map.55 = bf16[448,5120]{1,0:T(8,128)(2,1)S(1)} custom-call(s32[8]{0:T(128)} %frames_ref.1, s32[8]{0:T(128)} %motion_ref.1, bf16[448,5120]{1,0:T(8,128)(2,1)} %q_ref.1, bf16[448,5120]{1,0:T(8,128)(2,1)} %k_ref.1, bf16[448,5120]{1,0:T(8,128)(2,1)} %v_ref.1), custom_call_target="tpu_custom_call" | custom-call | flops 12918456320 | bytes 18350080 | tf_op jit(solution)/shard_map/pallas_call | solution.py:287
  204.9 2.1 %copy.7 = bf16[448,5120]{1,0:T(8,128)(2,1)} copy(bf16[448,5120]{1,0:T(8,128)(2,1)S(1)} %shard_map.55) | data formatting | bytes 9175040

commit v5 on v4

--- a/solution.py
+++ b/solution.py
@@ -16,8 +16,8 @@
 MESH = pl.DeviceIdType.MESH
 
 PACK = 2
-AHEAD = 3
-LEAD = 1
+AHEAD = 4
+LEAD = 2
 LAG = 2
 
 

time: 207 us -> 207 us (level)
  no operation moved by 1% of the time
where the time goes in v5:
time: 207 us
  Pallas kernels  205 us (99%)
  local copies, waits for them, and re-layouts  2.15 us (1%)
    pallas_call x1, Pallas kernels, body(): pl.pallas_call(functools.partial(kernel, groups, stretches, count, pack,...  205 us

profile of v5, /device:TPU:0, one launch (start us, length us, event | category | flops | bytes accessed | tf_op | source)
XLA Modules:
  0.0 207.1 jit_solution(12446756074516646560)
XLA Ops:
  0.0 204.9 %shard_map.55 = bf16[448,5120]{1,0:T(8,128)(2,1)S(1)} custom-call(s32[8]{0:T(128)} %frames_ref.1, s32[8]{0:T(128)} %motion_ref.1, bf16[448,5120]{1,0:T(8,128)(2,1)} %q_ref.1, bf16[448,5120]{1,0:T(8,128)(2,1)} %k_ref.1, bf16[448,5120]{1,0:T(8,128)(2,1)} %v_ref.1), custom_call_target="tpu_custom_call" | custom-call | flops 12918456320 | bytes 18350080 | tf_op jit(solution)/shard_map/pallas_call | solution.py:287
  204.9 2.1 %copy.7 = bf16[448,5120]{1,0:T(8,128)(2,1)} copy(bf16[448,5120]{1,0:T(8,128)(2,1)S(1)} %shard_map.55) | data formatting | bytes 9175040

commit v6 on v4

--- a/solution.py
+++ b/solution.py
@@ -15,14 +15,14 @@
 NEG = -1e30
 MESH = pl.DeviceIdType.MESH
 
-PACK = 2
-AHEAD = 3
+PACK = 4
+AHEAD = 2
 LEAD = 1
-LAG = 2
+LAG = 1
 
 
 def kernel(
-    groups, stretches, count, pack, rows, sub,
+    groups, stretches, count, pack, rows, fine, sub,
     frames_ref, motion_ref, q_ref, k_ref, v_ref, out_ref,
     qb, kb, vb, kt, vt, ob, bias,
     in_send, in_recv, in_local, q_send, q_recv, out_send, out_recv, out_local, mot_send, mot_recv,
@@ -31,7 +31,6 @@
     tail = MOT_CAP * FT
     unit = pack * HD
     local = count * unit
-    fine = rows // sub
     me = lax.axis_index("head")
     stretch = lax.axis_index("stretch")
     has_after = stretch < stretches - 1
@@ -154,12 +153,12 @@
 
     scale = math.log2(math.e) / math.sqrt(HD)
 
-    def attend(index, base):
-        row = base + lax.broadcasted_iota(jnp.int32, (sub, 1), 0)
+    def attend(index, base, size):
+        row = base + lax.broadcasted_iota(jnp.int32, (size, 1), 0)
         for head in range(pack):
             lanes = slice(head * HD, (head + 1) * HD)
             scores = lax.dot_general(
-                qb[index, pl.ds(base, sub), lanes], kb[index, :, lanes],
+                qb[index, pl.ds(base, size), lanes], kb[index, :, lanes],
                 (((1,), (1,)), ((), ())), preferred_element_type=jnp.float32,
             )
             scores = scores * scale + bias[...]
@@ -171,14 +170,16 @@
                 preferred_element_type=jnp.float32,
             )
             mixed = jnp.where(row < live_frames * FT, acc / total, 0.0)
-            ob[index, pl.ds(base, sub), lanes] = mixed.astype(jnp.bfloat16)
+            ob[index, pl.ds(base, size), lanes] = mixed.astype(jnp.bfloat16)
 
     def attend_rows(index, begin, number):
+        size = min(sub, number)
+
         def block(step, carry):
-            attend(index, pl.multiple_of(begin + step * sub, 16))
+            attend(index, pl.multiple_of(begin + step * size, 16), size)
             return carry
 
-        lax.fori_loop(0, number, block, 0)
+        lax.fori_loop(0, number // size, block, 0)
 
     barrier = pltpu.get_barrier_semaphore()
     for offset in range(1, groups):
@@ -226,14 +227,14 @@
                 pass_on(which, index).wait_recv()
 
         keep(2, index).wait()
-        attend_rows(index, me * rows, fine)
+        attend_rows(index, me * rows, rows)
         own_output(index).start()
         for offset in range(1, groups):
             to = peer(offset)
 
             def chunk(part, carry):
                 query(index, groups - offset, to, part, parts).wait_recv()
-                attend_rows(index, to * rows + part * (rows // parts), fine // parts)
+                attend_rows(index, to * rows + part * (rows // parts), rows // parts)
                 give_back(index, offset, None, part, parts).start()
                 return carry
 
@@ -281,11 +282,11 @@
     count = heads // pack
     unit = pack * HD
     sub = rows // 4 if rows % 64 == 0 else rows
-    fine = rows // sub
+    fine = rows // 64 if rows % 64 == 0 else 1
     wide = jnp.bfloat16
     dma = pltpu.SemaphoreType.DMA
     return pl.pallas_call(
-        functools.partial(kernel, groups, stretches, count, pack, rows, sub),
+        functools.partial(kernel, groups, stretches, count, pack, rows, fine, sub),
         out_shape=pltpu.VMEM((rows, width), wide),
         in_specs=[pl.BlockSpec(memory_space=pltpu.SMEM)] * 2
         + [pl.BlockSpec(memory_space=pltpu.HBM)] * 3,

time: 207 us -> 207 us (level)
  no operation moved by 1% of the time
where the time goes in v6:
time: 207 us; the launch traced here: 206 us
  Pallas kernels  204 us (99%)
  local copies, waits for them, and re-layouts  2.15 us (1%)
    pallas_call x1, Pallas kernels, body(): pl.pallas_call(functools.partial(kernel, groups, stretches, count, pack,...  204 us

profile of v6, /device:TPU:0, one launch (start us, length us, event | category | flops | bytes accessed | tf_op | source)
XLA Modules:
  0.0 206.3 jit_solution(9204976491979273685)
XLA Ops:
  0.0 204.2 %shard_map.55 = bf16[448,5120]{1,0:T(8,128)(2,1)S(1)} custom-call(s32[8]{0:T(128)} %frames_ref.1, s32[8]{0:T(128)} %motion_ref.1, bf16[448,5120]{1,0:T(8,128)(2,1)} %q_ref.1, bf16[448,5120]{1,0:T(8,128)(2,1)} %k_ref.1, bf16[448,5120]{1,0:T(8,128)(2,1)} %v_ref.1), custom_call_target="tpu_custom_call" | custom-call | flops 12918456320 | bytes 18350080 | tf_op jit(solution)/shard_map/pallas_call | solution.py:288
  204.2 2.1 %copy.7 = bf16[448,5120]{1,0:T(8,128)(2,1)} copy(bf16[448,5120]{1,0:T(8,128)(2,1)S(1)} %shard_map.55) | data formatting | bytes 9175040

commit v7 on v6

--- a/solution.py
+++ b/solution.py
@@ -16,8 +16,8 @@
 MESH = pl.DeviceIdType.MESH
 
 PACK = 4
-AHEAD = 2
-LEAD = 1
+AHEAD = 3
+LEAD = 2
 LAG = 1
 
 
@@ -272,6 +272,19 @@
     retire(jnp.int32(count - 1), fine)
 
 
+def store(pieces, held, out_ref, sems):
+    size = held.shape[0] // pieces
+
+    def piece(index):
+        part = pl.ds(index * size, size)
+        return pltpu.make_async_copy(held.at[part, :], out_ref.at[part, :], sems.at[index])
+
+    for index in range(pieces):
+        piece(index).start()
+    for index in range(pieces):
+        piece(index).wait()
+
+
 def body(groups, stretches, queries, keys, values, frames, motion):
     rows, width = queries.shape
     span = rows * groups
@@ -281,11 +294,12 @@
     pack = math.gcd(heads, PACK)
     count = heads // pack
     unit = pack * HD
-    sub = rows // 4 if rows % 64 == 0 else rows
+    sub = rows // 2 if rows % 64 == 0 else rows
     fine = rows // 64 if rows % 64 == 0 else 1
+    pieces = 7
     wide = jnp.bfloat16
     dma = pltpu.SemaphoreType.DMA
-    return pl.pallas_call(
+    result = pl.pallas_call(
         functools.partial(kernel, groups, stretches, count, pack, rows, fine, sub),
         out_shape=pltpu.VMEM((rows, width), wide),
         in_specs=[pl.BlockSpec(memory_space=pltpu.SMEM)] * 2
@@ -319,6 +333,17 @@
             transcendentals=span * (span + tail) * heads,
         ),
     )(frames, motion, queries, keys, values)
+    return pl.pallas_call(
+        functools.partial(store, pieces),
+        out_shape=jax.ShapeDtypeStruct((rows, width), wide),
+        in_specs=[pl.BlockSpec(memory_space=pltpu.VMEM)],
+        out_specs=pl.BlockSpec(memory_space=pltpu.HBM),
+        scratch_shapes=[dma((pieces,))],
+        compiler_params=pltpu.CompilerParams(vmem_limit_bytes=16 * 1024 * 1024),
+        cost_estimate=pl.CostEstimate(
+            flops=0, bytes_accessed=4 * rows * width, transcendentals=0
+        ),
+    )(result)
 
 
 def solution(mesh):

time: 207 us -> 207 us (level)
  local copies, waits for them, and re-layouts: 2.15 us -> 0 us
    pallas_call x0 -> x1, Pallas kernels: none -> 2.19 us  [body(): pl.pallas_call(functools.partial(store, pieces), out_shape=jax.ShapeDtype...]
    unnamed x1 -> x0, local copies, waits for them, and re-layouts: 2.15 us -> none
where the time goes in v7:
time: 207 us; the launch traced here: 206 us
  Pallas kernels  206 us (100%)
    pallas_call x1, Pallas kernels, body(): pl.pallas_call(functools.partial(kernel, groups, stretches, count, pack,...  204 us

profile of v7, /device:TPU:0, one launch (start us, length us, event | category | flops | bytes accessed | tf_op | source)
XLA Modules:
  0.0 206.4 jit_solution(1862804015009475016)
XLA Ops:
  0.0 204.2 %shard_map.55.held = bf16[448,5120]{1,0:T(8,128)(2,1)S(1)} custom-call(s32[8]{0:T(128)} %frames_ref.1, s32[8]{0:T(128)} %motion_ref.1, bf16[448,5120]{1,0:T(8,128)(2,1)} %q_ref.1, bf16[448,5120]{1,0:T(8,128)(2,1)} %k_ref.1, bf16[448,5120]{1,0:T(8,128)(2,1)} %v_ref.1), custom_call_target="tpu_custom_call" | custom-call | flops 12918456320 | bytes 18350080 | tf_op jit(solution)/shard_map/pallas_call | solution.py:302
  204.2 2.2 %shard_map.56 = bf16[448,5120]{1,0:T(8,128)(2,1)} custom-call(bf16[448,5120]{1,0:T(8,128)(2,1)S(1)} %shard_map.55.held), custom_call_target="tpu_custom_call" | custom-call | bytes 9175040 | tf_op jit(solution)/shard_map/pallas_call | solution.py:336
